TPU v7x, 32 devices: a whole 2x2x4 slice. The times are simulated.
32 devices in a mesh: query: 2 (over y), tok: 2 (over core), row: 4 (over z), col: 2 (over x).
Axes of the slice: x: 2, y: 2, z: 4, core: 2. Of those that a mesh axis runs over, the one named last changes fastest.
Arguments:
- activations: bfloat16 [128, 2560], P(('query', 'row'), ('tok', 'col')), parts along dimension 0, may hold values from -6 to 6
- out_grads: bfloat16 [128, 6912], P(('query', 'tok', 'col'), 'row'), parts along dimension 0, may hold values from -6 to 6
- left_basis: float32 [2560, 2560], P(('tok', 'col'), 'row'), may hold values from -0.125 to 0.125
- right_basis: float32 [6912, 6912], P('row', ('tok', 'col')), may hold values from -0.078125 to 0.078125
- spectrum: float32 [2560, 6912], P('row', ('tok', 'col')), may hold values from 0.005 to 0.1
Outputs:
- preconditioned: float32 [5120, 6912], P(('query', 'tok', 'col'), 'row'), parts along dimension 0
There are 2 independent parts, one for each index of `query`. A program takes and returns all parts, laid end to end along the dimension named above; an argument that names none is the same for every part. Nothing has to cross between parts.
All inputs are finite; a program needn't handle non-finite values.
Results may differ from a plain program's by a relative error of at most 0.003.
Values may be sent and summed in bfloat16 or wider, within the bound.
A program may use at most 128 MiB of HBM per device.

v0:
```python
import jax
import jax.numpy as jnp
from jax import lax
from jax.sharding import PartitionSpec as P

DAMPING = 0.002


def product(left, right):
    return jnp.dot(left, right, precision=lax.Precision.HIGHEST, preferred_element_type=jnp.float32)


def full_left(left_basis):
    return lax.all_gather(left_basis, "row", axis=1, tiled=True)


def shards(activations, out_grads, left_basis, right_basis, spectrum):
    grad_part = product(
        lax.all_gather(out_grads, ("tok", "col"), axis=0, tiled=True).astype(jnp.float32),
        right_basis,
    )
    rotated_grads = lax.psum(grad_part, "row")
    act_part = product(
        lax.all_gather(activations, "row", axis=0, tiled=True).astype(jnp.float32), left_basis
    )
    rotated_acts = lax.psum(act_part, ("tok", "col"))
    token_count = rotated_grads.shape[0]
    rotated = product(rotated_acts.T, rotated_grads) / token_count
    scaled = (rotated / (spectrum + DAMPING)).astype(jnp.bfloat16)
    right_turned = right_basis.T
    back_part = product(
        lax.all_gather(scaled, "row", axis=0, tiled=True).astype(jnp.float32), right_turned
    )
    back = lax.psum(back_part, ("tok", "col")).astype(jnp.bfloat16)
    left_rows = full_left(left_basis)
    return product(left_rows, back.astype(jnp.float32))


def solution(mesh):
    return jax.shard_map(
        shards,
        mesh=mesh,
        in_specs=(
            P(("query", "row"), ("tok", "col")),
            P(("query", "tok", "col"), "row"),
            P(("tok", "col"), "row"),
            P("row", ("tok", "col")),
            P("row", ("tok", "col")),
        ),
        out_specs=P(("query", "tok", "col"), "row"),
        check_vma=False,
    )
```

profile of v0, /device:TPU:0, one launch (start us, length us, event | category | flops | bytes accessed | tf_op | source)
XLA Modules:
  0.0 988.2 jit_solution(9545943735184302176)
XLA Ops:
  6.5 0.0 all-reduce.4.cloned.1.call-start
  6.5 15.1 %all_gather.12 = bf16[64,640]{1,0:T(8,128)(2,1)S(1)} all-gather(bf16[16,640]{1,0:T(8,128)(2,1)} %param.5), channel_id=1, replica_groups=mesh['query'=2,'tok'=2,'row'=4,'col'=2] {'row'}, dimensions={0}, use_global_device_ids=true | all-gather | bytes 102400 | tf_op jit(solution)/shard_map/all_gather | solution.py:24
  21.6 2.8 fusion.5
  24.4 0.0 all-reduce.4.cloned.1.call-update
  24.4 0.0 all-reduce.6.cloned.1.call-start
  24.5 10.7 %all_gather.13 = bf16[64,1728]{1,0:T(8,128)(2,1)S(1)} all-gather(bf16[16,1728]{1,0:T(8,128)(2,1)} %param.6), channel_id=1, replica_groups=mesh['query'=2,'tok'=2,'row'=4,'col'=2] {'tok','col'}, dimensions={0}, use_global_device_ids=true | all-gather | bytes 276480 | tf_op jit(solution)/shard_map/all_gather | solution.py:19
  35.2 8.5 fusion.6
  43.7 0.0 all-reduce.6.cloned.1.call-update
  43.7 0.0 all-gather.3.cloned.1.call-start
  43.8 13.6 %all-reduce.4.cloned.1.call-done = f32[64,640]{1,0:T(8,128)} async-done(((f32[64,640]{1,0:T(8,128)}), f32[64,640]{1,0:T(8,128)}) %all-reduce.4.cloned.1.call-update) | async-done | bytes 163856 | tf_op jit(solution)/shard_map/psum | solution.py:26
  57.4 40.0 %all-reduce.6.cloned.1.call-done = f32[64,1728]{1,0:T(8,128)} async-done(((f32[64,1728]{1,0:T(8,128)}), f32[64,1728]{1,0:T(8,128)}) %all-reduce.6.cloned.1.call-update) | async-done | bytes 442384 | tf_op jit(solution)/shard_map/psum | solution.py:22
  97.4 8.0 divide_convert_fusion
  105.4 0.0 all-gather.3.cloned.1.call-update
  105.4 0.0 all-gather.5.cloned.1.call-start
  105.5 0.5 all-gather.5.cloned.1.call-update
  106.0 156.5 %all-gather.3.cloned.1.call-done = bf16[2560,1728]{0,1:T(8,128)(2,1)} async-done(((bf16[640,1728]{0,1:T(8,128)(2,1)}), bf16[2560,1728]{0,1:T(8,128)(2,1)}) %all-gather.3.cloned.1.call-update) | async-done | bytes 8847376 | tf_op jit(solution)/shard_map/all_gather | solution.py:32
  262.5 80.1 %fusion.7 = f32[2560,1728]{1,0:T(8,128)} fusion(bf16[2560,1728]{0,1:T(8,128)(2,1)} %all-gather.3.cloned.1.call-done, f32[1728,1728]{1,0:T(8,128)} %param.8), kind=kOutput, calls=%fused_computation.6 | convolution fusion | flops 91729428480 | bytes 38486016 | tf_op jit(solution)/shard_map/dot_general | solution.py:10
  342.6 609.0 %all-reduce.7 = bf16[2560,1728]{1,0:T(8,128)(2,1)} all-reduce(f32[2560,1728]{1,0:T(8,128)} %fusion.7), channel_id=1, replica_groups=mesh['query'=2,'tok'=2,'row'=4,'col'=2] {'tok','col'}, use_global_device_ids=true, to_apply=%region_2.0 | all-reduce | flops 4423680 | bytes 26542080 | tf_op jit(solution)/shard_map/psum | solution.py:34
  951.6 0.0 all-gather.5.cloned.1.call-done
  951.6 30.1 %fusion.2 = f32[640,1728]{0,1:T(8,128)} fusion(f32[640,2560]{1,0:T(8,128)} %all-gather.5.cloned.1.call-done, bf16[2560,1728]{1,0:T(8,128)(2,1)} %all-reduce.7), kind=kOutput, calls=%fused_computation.3 | convolution fusion | flops 33973862400 | bytes 19824640 | tf_op jit(solution)/shard_map/dot_general | solution.py:10
Async XLA Ops:
  6.5 50.8 %all-reduce.4.cloned.1.call-start = ((), (), s32[]{:S(2)}) async-start(), calls=%async_computation | async-start | bytes 327680 | tf_op jit(solution)/shard_map/psum | solution.py:26
  24.4 73.0 %all-reduce.6.cloned.1.call-start = ((), (), s32[]{:S(2)}) async-start(), calls=%async_computation.1 | async-start | bytes 917504 | tf_op jit(solution)/shard_map/psum | solution.py:22
  43.7 218.8 %all-gather.3.cloned.1.call-start = ((), (), s32[]{:S(2)}) async-start(), calls=%async_computation.2 | async-start | bytes 11059200 | tf_op jit(solution)/shard_map/all_gather | solution.py:32
  105.4 846.1 %all-gather.5.cloned.1.call-start = ((), (), s32[]{:S(2)}) async-start(), calls=%async_computation.3 | async-start | bytes 8192000 | tf_op jit(solution)/shard_map/all_gather | solution.py:14
Sparse Core Ops, SparseCore 0:
  24.6 32.7 all-reduce.3
  59.9 37.5 all-reduce.5
  105.5 156.9 all-gather.2
  264.0 117.8 all-gather.4
where the time goes:
time: 988 us
  blocking collectives  635 us (64%)
  waiting for transfers between devices  211 us (21%)
  matrix products  129 us (13%)
  between operations  13.1 us (1%)
    psum x1, blocking collectives, shards(): back = lax.psum(back_part, ('tok', 'col')).astype(jnp.bfloat16)  609 us
    all_gather x1, waiting for transfers between devices, shards(): lax.all_gather(scaled, 'row', axis=0, tiled=True).astype(jnp.float32)  157 us
    dot_general x5, matrix products, product(): jnp.dot(left, right, precision=lax.Precision.HIGHEST, preferred_element_t...  129 us
    psum x1, waiting for transfers between devices, shards(): rotated_grads = lax.psum(grad_part, 'row')  40 us
  transfers between devices with their start and end apart: 4, of which 3 were waited for; matrix products, arithmetic and copies ran while one was open for 9% of the time, Pallas kernels for 0%

commit v1 on v0

v1 whole, which is shorter than its diff:
```python
import jax
import jax.numpy as jnp
from jax import lax
from jax.sharding import PartitionSpec as P

DAMPING = 0.002
F32, BF16, F16 = jnp.float32, jnp.bfloat16, jnp.float16


def shift(x, axis, n, s):
    return lax.ppermute(x, axis, [(i, (i + s) % n) for i in range(n)])


def gather(x, axis, n):
    me = lax.axis_index(axis)
    if n == 2:
        other = shift(x, axis, n, 1)
        return jnp.stack([jnp.where(me == 0, x, other), jnp.where(me == 0, other, x)])
    out = jnp.zeros((n,) + x.shape, x.dtype)
    out = lax.dynamic_update_index_in_dim(out, x, me, 0)
    for s in range(1, n):
        out = lax.dynamic_update_index_in_dim(out, shift(x, axis, n, s), (me - s) % n, 0)
    return out


def exchange_sum(x, axis, n, sent=F32):
    total = x
    for s in range(1, n):
        total = total + shift(x.astype(sent), axis, n, s).astype(F32)
    return total


def scatter_sum(x, axis, n):
    me = lax.axis_index(axis)
    total = lax.dynamic_index_in_dim(x, me, 0, keepdims=False)
    for s in range(1, n):
        part = lax.dynamic_index_in_dim(x, (me + s) % n, 0, keepdims=False)
        total = total + shift(part, axis, n, s)
    return total


def narrow(left, right, dims):
    return lax.dot_general(left, right, (dims, ((), ())), preferred_element_type=F32)


def wide(left, right):
    return jnp.dot(left, right, precision=lax.Precision.HIGH, preferred_element_type=F32)


def halves(x):
    high = lax.reduce_precision(x, 8, 7)
    return high.astype(BF16), (x - high).astype(BF16)


def shards(sizes, activations, out_grads, left_basis, right_basis, spectrum):
    nq, nt, nr, nc = (sizes[a] for a in ("query", "tok", "row", "col"))
    query, row, tok = (lax.axis_index(a) for a in ("query", "row", "tok"))
    block, width = spectrum.shape

    share = block // nq
    ring = lax.dynamic_slice_in_dim(spectrum, query * share, share, 0).astype(F16)
    spectra = [spectrum]
    for _ in range(1, nr):
        ring = shift(ring, "row", nr, 1)
        spectra.append(gather(ring, "query", nq).reshape(block, width))

    grads = gather(gather(out_grads, "col", nc), "tok", nt).reshape(-1, out_grads.shape[1])
    grads = wide(grads.astype(F32), right_basis)
    tokens = grads.shape[0]
    grads = scatter_sum(grads.reshape(nr, tokens // nr, width), "row", nr)
    grads = gather(grads, "row", nr).reshape(tokens, width) * (1.0 / tokens)
    high, low = halves(grads)
    grads = jnp.concatenate([high, low, high], 0)

    acts = gather(activations, "row", nr).reshape(tokens, -1)
    acts = wide(acts.astype(F32), left_basis)
    acts = exchange_sum(exchange_sum(acts, "tok", nt), "col", nc)
    acts = [acts] + [shift(acts, "row", nr, s) for s in range(1, nr)]

    lefts = [left_basis.astype(BF16)]
    for _ in range(1, nr):
        lefts.append(shift(lefts[-1], "row", nr, 1))

    right = right_basis.astype(BF16)
    half = block // nt
    out = None
    for s in range(nr):
        high, low = halves(acts[s])
        rotated = narrow(jnp.concatenate([high, high, low], 0), grads, ((0,), (0,)))
        scaled = (rotated / (spectra[s].astype(F32) + DAMPING)).astype(BF16)
        part = narrow(scaled, right, ((1,), (1,))).reshape(nt, half, -1)
        back = scatter_sum(part, "tok", nt)
        back = exchange_sum(back, "col", nc, BF16).astype(BF16)
        back = gather(back, "tok", nt).reshape(block, -1)
        term = narrow(lefts[s], back, ((1,), (0,)))
        out = term if out is None else out + term
    return out


def solution(mesh):
    sizes = dict(mesh.shape)
    return jax.shard_map(
        lambda *args: shards(sizes, *args),
        mesh=mesh,
        in_specs=(
            P(("query", "row"), ("tok", "col")),
            P(("query", "tok", "col"), "row"),
            P(("tok", "col"), "row"),
            P("row", ("tok", "col")),
            P("row", ("tok", "col")),
        ),
        out_specs=P(("query", "tok", "col"), "row"),
        check_vma=False,
    )
```

time: 988 us -> 349 us (0.35)
  blocking collectives: 635 us -> 0 us
  waiting for transfers between devices: 211 us -> 114 us
  starting transfers between devices: 0.13 us -> 75.5 us
  matrix products: 129 us -> 73.4 us
  other arithmetic: 0 us -> 45.1 us
  local copies, waits for them, and re-layouts: 0 us -> 34.1 us
  between operations: 13.1 us -> 0.79 us
    psum x1 -> x0, blocking collectives: 609 us -> none  [shards(): back = lax.psum(back_part, ('tok', 'col')).astype(jnp.bfloat16)]
    all_gather x2 -> x0, waiting for transfers between devices: 157 us -> none  [the longest x1 157 us: shards(): lax.all_gather(scaled, 'row', axis=0, tiled=True).astype(jnp.float32)]
    ppermute x0 -> x37, waiting for transfers between devices: none -> 114 us  [shift(): return lax.ppermute(x, axis, [(i, (i + s) % n) for i in range(n)])]
    ppermute x0 -> x37, starting transfers between devices: none -> 75.5 us  [shift(): return lax.ppermute(x, axis, [(i, (i + s) % n) for i in range(n)])]
    dot_general x5 -> x10, matrix products: 129 us -> 73.4 us  [the longest x8 64.4 us: narrow(): lax.dot_general(left, right, (dims, ((), ())), preferred_element_type=F32)]
    psum x2 -> x0, waiting for transfers between devices: 53.7 us -> none  [the longest x1 40 us: shards(): rotated_grads = lax.psum(grad_part, 'row')]
    convert_element_type x0 -> x17, other arithmetic: none -> 26.8 us  [the longest x4 7.97 us: exchange_sum(): total = total + shift(x.astype(sent), axis, n, s).astype(F32)]
    all_gather x2 -> x0, blocking collectives: 25.8 us -> none  [the longest x1 15.1 us: shards(): lax.all_gather(activations, 'row', axis=0, tiled=True).astype(jnp.float32)]
  transfers between devices with their start and end apart: 4 -> 37, of which waited for: 3 -> 11; matrix products, arithmetic and copies ran while one was open for 9% -> 42% of each run, Pallas kernels for 0% -> 0%
where the time goes in v1:
time: 349 us; the launch traced here: 343 us
  waiting for transfers between devices  114 us (33%)
  starting transfers between devices  75.5 us (22%)
  matrix products  73.4 us (21%)
  other arithmetic  45.1 us (13%)
  local copies, waits for them, and re-layouts  34.1 us (10%)
    ppermute x37, waiting for transfers between devices, shift(): return lax.ppermute(x, axis, [(i, (i + s) % n) for i in range(n)])  114 us
    ppermute x37, starting transfers between devices, shift(): return lax.ppermute(x, axis, [(i, (i + s) % n) for i in range(n)])  75.5 us
    dot_general x8, matrix products, narrow(): lax.dot_general(left, right, (dims, ((), ())), preferred_element_type=F32)  64.4 us
    add x3, local copies, waits for them, and re-layouts, shards(): scaled = (rotated / (spectra[s].astype(F32) + DAMPING)).astype(BF16)  17 us
    squeeze x5, local copies, waits for them, and re-layouts, scatter_sum(): part = lax.dynamic_index_in_dim(x, (me + s) % n, 0, keepdims=False)  12.2 us
    another operation x15, other arithmetic, gather(): jnp.stack([jnp.where(me == 0, x, other), jnp.where(me == 0, other, x)])  9.37 us
    dot_general x2, matrix products, wide(): jnp.dot(left, right, precision=lax.Precision.HIGH, preferred_element_type...  9.04 us
    convert_element_type x4, other arithmetic, exchange_sum(): total = total + shift(x.astype(sent), axis, n, s).astype(F32)  7.97 us
  transfers between devices with their start and end apart: 37, of which 11 were waited for; matrix products, arithmetic and copies ran while one was open for 42% of the time, Pallas kernels for 0%

profile of v1, /device:TPU:0, one launch (start us, length us, event | category | flops | bytes accessed | tf_op | source)
XLA Modules:
  0.0 342.8 jit_solution(3482364709879275800)
XLA Ops:
  14.8 7.2 %fusion = f32[4,16,1728]{2,1,0:T(8,128)S(1)} fusion(bf16[4,16,1728]{2,1,0:T(8,128)(2,1)S(1)} %bitcast.160, f32[1728,1728]{1,0:T(8,128)} %param.8), kind=kOutput, calls=%fused_computation | convolution fusion | flops 1146617856 | bytes 12607488 | tf_op jit(solution)/shard_map/dot_general | solution.py:47
  32.9 7.8 %convert_element_type.106 = bf16[1728,1728]{1,0:T(8,128)(2,1)} convert(f32[1728,1728]{1,0:T(8,128)} %param.8) | non-fusion elementwise | flops 2985984 | bytes 17915904 | tf_op jit(solution)/shard_map/convert_element_type | solution.py:84
  45.6 38.9 %collective-permute-start.10 = (f32[16,1728]{1,0:T(8,128)S(1)}, f32[16,1728]{1,0:T(8,128)S(1)}, u32[]{:S(2)}, u32[]{:S(2)}) collective-permute-start(f32[16,1728]{1,0:T(8,128)S(1)} %get-tuple-element.8), channel_id=1, source_target_pairs={{0,2},{2,4},{4,6},{6,0},{1,3},{3,5},{5,7},{7,1},{8,10},{10,12},{12... | collective-permute-start | bytes 331784 | tf_op jit(solution)/shard_map/ppermute | solution.py:11
  89.1 6.1 %collective-permute-done.11 = f32[16,1728]{1,0:T(8,128)S(1)} collective-permute-done((f32[16,1728]{1,0:T(8,128)S(1)}, f32[16,1728]{1,0:T(8,128)S(1)}, u32[]{:S(2)}, u32[]{:S(2)}) %collective-permute-start.11) | collective-permute-done | bytes 110624 | tf_op jit(solution)/shard_map/ppermute | solution.py:11
  100.3 12.1 %fusion.5 = f32[640,1728]{1,0:T(8,128)} fusion(bf16[1728,1728]{1,0:T(8,128)(2,1)} %convert_element_type.106, f32[640,1728]{0,1:T(8,128)} %param.9, bf16[64,640]{1,0:T(8,128)(2,1)S(1)} %fusion.51, bf16[64,640]{1,0:T(8,128)(2,1)S(1)} %get-tuple-element.5, bf16[64,1728]{1,0:T(8,128)(2,1)S(1)} %get-tuple-element.24, bf16[64,1728]{1,0:T(8,128)(2,1)S(1)} %get-tuple-element.23), kind=kOutput, calls=%fused_computation.29 | convolution fusion | flops 4252778496 | bytes 15425536 | tf_op jit(solution)/shard_map/dot_general | solution.py:43
  113.7 3.2 dynamic-slice_bitcast_fusion.3
  119.3 11.6 %collective-permute-done.29 = bf16[640,640]{1,0:T(8,128)(2,1)} collective-permute-done((bf16[640,640]{1,0:T(8,128)(2,1)}, bf16[640,640]{1,0:T(8,128)(2,1)}, u32[]{:S(2)}, u32[]{:S(2)}) %collective-permute-start.29) | collective-permute-done | bytes 819232 | tf_op jit(solution)/shard_map/ppermute | solution.py:11
  136.0 5.6 %copy.15 = f32[640,1728]{0,1:T(8,128)} copy(f32[640,1728]{1,0:T(8,128)} %bitcast.133) | data formatting | bytes 8847360 | tf_op jit(solution)/shard_map/add | solution.py:90
  141.7 13.6 %collective-permute-done.24 = f16[320,1728]{1,0:T(8,128)(2,1)S(1)} collective-permute-done((f16[320,1728]{1,0:T(8,128)(2,1)}, f16[320,1728]{1,0:T(8,128)(2,1)S(1)}, u32[]{:S(2)}, u32[]{:S(2)}) %collective-permute-start.24) | collective-permute-done | bytes 1105952 | tf_op jit(solution)/shard_map/ppermute | solution.py:11
  155.8 12.2 %fusion.2 = f32[640,1728]{1,0:T(8,128)} fusion(bf16[1728,1728]{1,0:T(8,128)(2,1)} %convert_element_type.106, f32[640,1728]{0,1:T(8,128)} %copy.15, bf16[64,640]{1,0:T(8,128)(2,1)S(1)} %get-tuple-element.33, bf16[64,640]{1,0:T(8,128)(2,1)S(1)} %get-tuple-element.32, bf16[64,1728]{1,0:T(8,128)(2,1)S(1)} %copy-done.5, bf16[64,1728]{1,0:T(8,128)(2,1)S(1)} %get-tuple-element.23), kind=kOutput, calls=%fused_computation.26 | convolution fusion | flops 4251672576 | bytes 15425536 | tf_op jit(solution)/shard_map/dot_general | solution.py:43
  172.2 3.6 %fusion.6 = bf16[320,1728]{1,0:T(8,128)(2,1)} fusion(f32[320,1728]{1,0:T(8,128)} %collective-permute-done.13, f32[2,320,1728]{2,1,0:T(8,128)} %bitcast.142, s32[]{:T(128)S(6)} %select_n.196), kind=kLoop, calls=%fused_computation.44 | loop fusion | flops 1105920 | bytes 5529604 | tf_op jit(solution)/shard_map/convert_element_type | solution.py:29
  181.6 5.6 %copy.17 = f32[640,1728]{0,1:T(8,128)} copy(f32[640,1728]{1,0:T(8,128)} %bitcast.134) | data formatting | bytes 8847360 | tf_op jit(solution)/shard_map/add | solution.py:90
  187.2 14.0 %collective-permute-done.31 = f16[320,1728]{1,0:T(8,128)(2,1)} collective-permute-done((f16[320,1728]{1,0:T(8,128)(2,1)S(1)}, f16[320,1728]{1,0:T(8,128)(2,1)}, u32[]{:S(2)}, u32[]{:S(2)}) %collective-permute-start.31) | collective-permute-done | bytes 1105952 | tf_op jit(solution)/shard_map/ppermute | solution.py:11
  202.8 12.5 %fusion.3 = f32[640,1728]{1,0:T(8,128)} fusion(bf16[1728,1728]{1,0:T(8,128)(2,1)} %convert_element_type.106, f32[640,1728]{0,1:T(8,128)} %copy.17, bf16[64,640]{1,0:T(8,128)(2,1)} %get-tuple-element.35, bf16[64,640]{1,0:T(8,128)(2,1)} %get-tuple-element.34, bf16[64,1728]{1,0:T(8,128)(2,1)} %copy-done.4, bf16[64,1728]{1,0:T(8,128)(2,1)} %copy-done.3), kind=kOutput, calls=%fused_computation.27 | convolution fusion | flops 4251672576 | bytes 15425536 | tf_op jit(solution)/shard_map/dot_general | solution.py:43
  215.3 3.3 dynamic-slice_bitcast_fusion.1
  222.2 6.3 %collective-permute-done.32 = f16[320,1728]{1,0:T(8,128)(2,1)} collective-permute-done((f16[320,1728]{1,0:T(8,128)(2,1)}, f16[320,1728]{1,0:T(8,128)(2,1)}, u32[]{:S(2)}, u32[]{:S(2)}) %collective-permute-start.32) | collective-permute-done | bytes 1105952 | tf_op jit(solution)/shard_map/ppermute | solution.py:11
  233.2 5.8 %copy.19 = f32[640,1728]{0,1:T(8,128)} copy(f32[640,1728]{1,0:T(8,128)} %bitcast.135) | data formatting | bytes 8847360 | tf_op jit(solution)/shard_map/add | solution.py:90
  238.9 12.5 %fusion.4 = f32[640,1728]{1,0:T(8,128)} fusion(bf16[1728,1728]{1,0:T(8,128)(2,1)} %convert_element_type.106, f32[640,1728]{0,1:T(8,128)} %copy.19, bf16[64,640]{1,0:T(8,128)(2,1)} %get-tuple-element.31, bf16[64,640]{1,0:T(8,128)(2,1)S(1)} %get-tuple-element.30, bf16[64,1728]{1,0:T(8,128)(2,1)} %copy-done.4, bf16[64,1728]{1,0:T(8,128)(2,1)} %copy-done.3), kind=kOutput, calls=%fused_computation.28 | convolution fusion | flops 4251672576 | bytes 15425536 | tf_op jit(solution)/shard_map/dot_general | solution.py:43
  264.6 18.6 %collective-permute-done.20 = bf16[320,1728]{1,0:T(8,128)(2,1)S(1)} collective-permute-done((bf16[320,1728]{1,0:T(8,128)(2,1)S(1)}, bf16[320,1728]{1,0:T(8,128)(2,1)S(1)}, u32[]{:S(2)}, u32[]{:S(2)}) %collective-permute-start.20) | collective-permute-done | bytes 1105952 | tf_op jit(solution)/shard_map/ppermute | solution.py:11
  285.5 22.3 %collective-permute-done.27 = bf16[320,1728]{1,0:T(8,128)(2,1)S(1)} collective-permute-done((bf16[320,1728]{1,0:T(8,128)(2,1)S(1)}, bf16[320,1728]{1,0:T(8,128)(2,1)S(1)}, u32[]{:S(2)}, u32[]{:S(2)}) %collective-permute-start.27) | collective-permute-done | bytes 1105952 | tf_op jit(solution)/shard_map/ppermute | solution.py:11
  310.3 3.6 %fusion.69 = f32[1728,640]{1,0:T(8,128)S(1)} fusion(bf16[640,1728]{1,0:T(8,128)(2,1)S(1)} %bitcast.156, bf16[640,640]{1,0:T(8,128)(2,1)} %collective-permute-done.22), kind=kOutput, calls=%fused_computation.113 | convolution fusion | flops 1415577600 | bytes 7454720 | tf_op jit(solution)/shard_map/dot_general | solution.py:43
  313.9 18.1 %collective-permute-done.34 = bf16[320,1728]{1,0:T(8,128)(2,1)S(1)} collective-permute-done((bf16[320,1728]{1,0:T(8,128)(2,1)S(1)}, bf16[320,1728]{1,0:T(8,128)(2,1)S(1)}, u32[]{:S(2)}, u32[]{:S(2)}) %collective-permute-start.34) | collective-permute-done | bytes 1105952 | tf_op jit(solution)/shard_map/ppermute | solution.py:11
  332.8 3.4 fusion.70
  336.7 5.9 %add_bitcast_fusion = f32[640,1728]{0,1:T(8,128)} fusion(f32[1728,640]{1,0:T(8,128)S(1)} %fusion.70, f32[1728,640]{1,0:T(8,128)S(1)} %fusion.68, f32[1728,640]{1,0:T(8,128)S(1)} %fusion.69, bf16[640,1728]{1,0:T(8,128)(2,1)S(1)} %bitcast.154, bf16[640,640]{1,0:T(8,128)(2,1)} %collective-permute-done.36), kind=kOutput, calls=%fused_computation.5 | convolution fusion | flops 1418895360 | bytes 20725760 | tf_op jit(solution)/shard_map/dot_general | solution.py:43
  (149 shorter events, 88.1 us)
Async XLA Ops:
  14.1 26.7 %collective-permute-start.3 = (f32[64,640]{1,0:T(8,128)S(1)}, f32[64,640]{1,0:T(8,128)S(1)}, u32[]{:S(2)}, u32[]{:S(2)}) collective-permute-start(f32[64,640]{1,0:T(8,128)S(1)} %fusion.67), channel_id=1, source_target_pairs={{0,8},{8,0},{1,9},{9,1},{2,10},{10,2},{3,11},{11,3},{4,12},{12,4},... | collective-permute-start | bytes 491528 | tf_op jit(solution)/shard_map/ppermute | solution.py:11
  32.3 66.4 %collective-permute-start.17 = (f16[320,1728]{1,0:T(8,128)(2,1)}, f16[320,1728]{1,0:T(8,128)(2,1)}, u32[]{:S(2)}, u32[]{:S(2)}) collective-permute-start(f16[320,1728]{1,0:T(8,128)(2,1)} %convert_element_type.113), channel_id=1, source_target_pairs={{0,2},{2,4},{4,6},{6,0},{1,3},{3,5},{5,7},{7,1},{8,10},{10,12},{12... | collective-permute-start | bytes 3317768 | tf_op jit(solution)/shard_map/ppermute | solution.py:11
  40.9 71.6 %collective-permute-start.22 = (bf16[640,640]{1,0:T(8,128)(2,1)S(1)}, bf16[640,640]{1,0:T(8,128)(2,1)}, u32[]{:S(2)}, u32[]{:S(2)}) collective-permute-start(bf16[640,640]{1,0:T(8,128)(2,1)S(1)} %convert_element_type.110), channel_id=1, source_target_pairs={{0,2},{2,4},{4,6},{6,0},{1,3},{3,5},{5,7},{7,1},{8,10},{10,12},{12... | collective-permute-start | bytes 2457608 | tf_op jit(solution)/shard_map/ppermute | solution.py:11
  43.0 41.5 %collective-permute-start.4 = (f32[64,640]{1,0:T(8,128)S(1)}, f32[64,640]{1,0:T(8,128)S(1)}, u32[]{:S(2)}, u32[]{:S(2)}) collective-permute-start(f32[64,640]{1,0:T(8,128)S(1)} %add.172), channel_id=1, source_target_pairs={{0,1},{1,0},{2,3},{3,2},{4,5},{5,4},{6,7},{7,6},{8,9},{9,8},{10,11... | collective-permute-start | bytes 491528 | tf_op jit(solution)/shard_map/ppermute | solution.py:11
  45.6 42.5 %collective-permute-start.10 = (f32[16,1728]{1,0:T(8,128)S(1)}, f32[16,1728]{1,0:T(8,128)S(1)}, u32[]{:S(2)}, u32[]{:S(2)}) collective-permute-start(f32[16,1728]{1,0:T(8,128)S(1)} %get-tuple-element.8), channel_id=1, source_target_pairs={{0,2},{2,4},{4,6},{6,0},{1,3},{3,5},{5,7},{7,1},{8,10},{10,12},{12... | collective-permute-start | bytes 331784 | tf_op jit(solution)/shard_map/ppermute | solution.py:11
  88.0 28.9 %collective-permute-start.30 = (f32[64,640]{1,0:T(8,128)S(1)}, f32[64,640]{1,0:T(8,128)S(1)}, u32[]{:S(2)}, u32[]{:S(2)}) collective-permute-start(f32[64,640]{1,0:T(8,128)S(1)} %get-tuple-element.6), channel_id=1, source_target_pairs={{0,6},{2,0},{4,2},{6,4},{1,7},{3,1},{5,3},{7,5},{8,14},{10,8},{12,... | collective-permute-start | bytes 491528 | tf_op jit(solution)/shard_map/ppermute | solution.py:11
  95.2 22.4 %collective-permute-start.16 = (f32[64,640]{1,0:T(8,128)S(1)}, f32[64,640]{1,0:T(8,128)S(1)}, u32[]{:S(2)}, u32[]{:S(2)}) collective-permute-start(f32[64,640]{1,0:T(8,128)S(1)} %get-tuple-element.6), channel_id=1, source_target_pairs={{0,2},{2,4},{4,6},{6,0},{1,3},{3,5},{5,7},{7,1},{8,10},{10,12},{12... | collective-permute-start | bytes 491528 | tf_op jit(solution)/shard_map/ppermute | solution.py:11
  95.4 22.2 %collective-permute-start.23 = (f32[64,640]{1,0:T(8,128)S(1)}, f32[64,640]{1,0:T(8,128)}, u32[]{:S(2)}, u32[]{:S(2)}) collective-permute-start(f32[64,640]{1,0:T(8,128)S(1)} %get-tuple-element.6), channel_id=1, source_target_pairs={{0,4},{2,6},{4,0},{6,2},{1,5},{3,7},{5,1},{7,3},{8,12},{10,14},{12... | collective-permute-start | bytes 491528 | tf_op jit(solution)/shard_map/ppermute | solution.py:11
  98.7 32.8 %collective-permute-start.18 = (f16[320,1728]{1,0:T(8,128)(2,1)}, f16[320,1728]{1,0:T(8,128)(2,1)S(1)}, u32[]{:S(2)}, u32[]{:S(2)}) collective-permute-start(f16[320,1728]{1,0:T(8,128)(2,1)} %collective-permute-done.17), channel_id=1, source_target_pairs={{0,16},{16,0},{1,17},{17,1},{2,18},{18,2},{3,19},{19,3},{4,20},{20... | collective-permute-start | bytes 3317768 | tf_op jit(solution)/shard_map/ppermute | solution.py:11
  116.9 55.2 %collective-permute-start.13 = (f32[320,1728]{1,0:T(8,128)}, f32[320,1728]{1,0:T(8,128)}, u32[]{:S(2)}, u32[]{:S(2)}) collective-permute-start(f32[320,1728]{1,0:T(8,128)} %dynamic-slice_bitcast_fusion.3), channel_id=1, source_target_pairs={{0,8},{8,0},{1,9},{9,1},{2,10},{10,2},{3,11},{11,3},{4,12},{12,4},... | collective-permute-start | bytes 6635528 | tf_op jit(solution)/shard_map/ppermute | solution.py:11
  117.6 37.7 %collective-permute-start.24 = (f16[320,1728]{1,0:T(8,128)(2,1)}, f16[320,1728]{1,0:T(8,128)(2,1)S(1)}, u32[]{:S(2)}, u32[]{:S(2)}) collective-permute-start(f16[320,1728]{1,0:T(8,128)(2,1)} %collective-permute-done.17), channel_id=1, source_target_pairs={{0,2},{2,4},{4,6},{6,0},{1,3},{3,5},{5,7},{7,1},{8,10},{10,12},{12... | collective-permute-start | bytes 3317768 | tf_op jit(solution)/shard_map/ppermute | solution.py:11
  130.8 205.8 %collective-permute-start.36 = (bf16[640,640]{1,0:T(8,128)(2,1)}, bf16[640,640]{1,0:T(8,128)(2,1)}, u32[]{:S(2)}, u32[]{:S(2)}) collective-permute-start(bf16[640,640]{1,0:T(8,128)(2,1)} %collective-permute-done.29), channel_id=1, source_target_pairs={{0,2},{2,4},{4,6},{6,0},{1,3},{3,5},{5,7},{7,1},{8,10},{10,12},{12... | collective-permute-start | bytes 2457608 | tf_op jit(solution)/shard_map/ppermute | solution.py:11
  171.2 82.1 %collective-permute-start.19 = (f32[320,1728]{1,0:T(8,128)}, f32[320,1728]{1,0:T(8,128)S(1)}, u32[]{:S(2)}, u32[]{:S(2)}) collective-permute-start(f32[320,1728]{1,0:T(8,128)} %dynamic-slice_bitcast_fusion.2), channel_id=1, source_target_pairs={{0,8},{8,0},{1,9},{9,1},{2,10},{10,2},{3,11},{11,3},{4,12},{12,4},... | collective-permute-start | bytes 6635528 | tf_op jit(solution)/shard_map/ppermute | solution.py:11
  171.2 30.0 %collective-permute-start.31 = (f16[320,1728]{1,0:T(8,128)(2,1)S(1)}, f16[320,1728]{1,0:T(8,128)(2,1)}, u32[]{:S(2)}, u32[]{:S(2)}) collective-permute-start(f16[320,1728]{1,0:T(8,128)(2,1)S(1)} %collective-permute-done.24), channel_id=1, source_target_pairs={{0,2},{2,4},{4,6},{6,0},{1,3},{3,5},{5,7},{7,1},{8,10},{10,12},{12... | collective-permute-start | bytes 3317768 | tf_op jit(solution)/shard_map/ppermute | solution.py:11
  175.7 42.9 %collective-permute-start.14 = (bf16[320,1728]{1,0:T(8,128)(2,1)}, bf16[320,1728]{1,0:T(8,128)(2,1)}, u32[]{:S(2)}, u32[]{:S(2)}) collective-permute-start(bf16[320,1728]{1,0:T(8,128)(2,1)} %fusion.6), channel_id=1, source_target_pairs={{0,1},{1,0},{2,3},{3,2},{4,5},{5,4},{6,7},{7,6},{8,9},{9,8},{10,11... | collective-permute-start | bytes 3317768 | tf_op jit(solution)/shard_map/ppermute | solution.py:11
  201.2 27.2 %collective-permute-start.32 = (f16[320,1728]{1,0:T(8,128)(2,1)}, f16[320,1728]{1,0:T(8,128)(2,1)}, u32[]{:S(2)}, u32[]{:S(2)}) collective-permute-start(f16[320,1728]{1,0:T(8,128)(2,1)} %collective-permute-done.31), channel_id=1, source_target_pairs={{0,16},{16,0},{1,17},{17,1},{2,18},{18,2},{3,19},{19,3},{4,20},{20... | collective-permute-start | bytes 3317768 | tf_op jit(solution)/shard_map/ppermute | solution.py:11
  218.6 42.1 %collective-permute-start.26 = (f32[320,1728]{1,0:T(8,128)}, f32[320,1728]{1,0:T(8,128)}, u32[]{:S(2)}, u32[]{:S(2)}) collective-permute-start(f32[320,1728]{1,0:T(8,128)} %dynamic-slice_bitcast_fusion.1), channel_id=1, source_target_pairs={{0,8},{8,0},{1,9},{9,1},{2,10},{10,2},{3,11},{11,3},{4,12},{12,4},... | collective-permute-start | bytes 6635528 | tf_op jit(solution)/shard_map/ppermute | solution.py:11
  221.6 35.1 %collective-permute-start.15 = (bf16[320,1728]{1,0:T(8,128)(2,1)S(1)}, bf16[320,1728]{1,0:T(8,128)(2,1)}, u32[]{:S(2)}, u32[]{:S(2)}) collective-permute-start(bf16[320,1728]{1,0:T(8,128)(2,1)S(1)} %add_convert_fusion.3), channel_id=1, source_target_pairs={{0,8},{8,0},{1,9},{9,1},{2,10},{10,2},{3,11},{11,3},{4,12},{12,4},... | collective-permute-start | bytes 3317768 | tf_op jit(solution)/shard_map/ppermute | solution.py:11
  253.2 30.5 %collective-permute-start.33 = (f32[320,1728]{1,0:T(8,128)S(1)}, f32[320,1728]{1,0:T(8,128)S(1)}, u32[]{:S(2)}, u32[]{:S(2)}) collective-permute-start(f32[320,1728]{1,0:T(8,128)S(1)} %dynamic-slice_bitcast_fusion), channel_id=1, source_target_pairs={{0,8},{8,0},{1,9},{9,1},{2,10},{10,2},{3,11},{11,3},{4,12},{12,4},... | collective-permute-start | bytes 6635528 | tf_op jit(solution)/shard_map/ppermute | solution.py:11
  255.1 28.1 %collective-permute-start.20 = (bf16[320,1728]{1,0:T(8,128)(2,1)S(1)}, bf16[320,1728]{1,0:T(8,128)(2,1)S(1)}, u32[]{:S(2)}, u32[]{:S(2)}) collective-permute-start(bf16[320,1728]{1,0:T(8,128)(2,1)S(1)} %fusion.7), channel_id=1, source_target_pairs={{0,1},{1,0},{2,3},{3,2},{4,5},{5,4},{6,7},{7,6},{8,9},{9,8},{10,11... | collective-permute-start | bytes 3317768 | tf_op jit(solution)/shard_map/ppermute | solution.py:11
  264.0 43.8 %collective-permute-start.27 = (bf16[320,1728]{1,0:T(8,128)(2,1)S(1)}, bf16[320,1728]{1,0:T(8,128)(2,1)S(1)}, u32[]{:S(2)}, u32[]{:S(2)}) collective-permute-start(bf16[320,1728]{1,0:T(8,128)(2,1)S(1)} %fusion.8), channel_id=1, source_target_pairs={{0,1},{1,0},{2,3},{3,2},{4,5},{5,4},{6,7},{7,6},{8,9},{9,8},{10,11... | collective-permute-start | bytes 3317768 | tf_op jit(solution)/shard_map/ppermute | solution.py:11
  283.6 26.3 %collective-permute-start.21 = (bf16[320,1728]{1,0:T(8,128)(2,1)S(1)}, bf16[320,1728]{1,0:T(8,128)(2,1)S(1)}, u32[]{:S(2)}, u32[]{:S(2)}) collective-permute-start(bf16[320,1728]{1,0:T(8,128)(2,1)S(1)} %add_convert_fusion.2), channel_id=1, source_target_pairs={{0,8},{8,0},{1,9},{9,1},{2,10},{10,2},{3,11},{11,3},{4,12},{12,4},... | collective-permute-start | bytes 3317768 | tf_op jit(solution)/shard_map/ppermute | solution.py:11
  284.0 48.1 %collective-permute-start.34 = (bf16[320,1728]{1,0:T(8,128)(2,1)S(1)}, bf16[320,1728]{1,0:T(8,128)(2,1)S(1)}, u32[]{:S(2)}, u32[]{:S(2)}) collective-permute-start(bf16[320,1728]{1,0:T(8,128)(2,1)S(1)} %fusion.9), channel_id=1, source_target_pairs={{0,1},{1,0},{2,3},{3,2},{4,5},{5,4},{6,7},{7,6},{8,9},{9,8},{10,11... | collective-permute-start | bytes 3317768 | tf_op jit(solution)/shard_map/ppermute | solution.py:11
  309.8 22.6 %collective-permute-start.28 = (bf16[320,1728]{1,0:T(8,128)(2,1)S(1)}, bf16[320,1728]{1,0:T(8,128)(2,1)S(1)}, u32[]{:S(2)}, u32[]{:S(2)}) collective-permute-start(bf16[320,1728]{1,0:T(8,128)(2,1)S(1)} %add_convert_fusion.1), channel_id=1, source_target_pairs={{0,8},{8,0},{1,9},{9,1},{2,10},{10,2},{3,11},{11,3},{4,12},{12,4},... | collective-permute-start | bytes 3317768 | tf_op jit(solution)/shard_map/ppermute | solution.py:11
  (27 other events, 438.9 us)
